TPU v7x, 32 devices: a whole 2x2x4 slice. The times are simulated.
32 devices in a mesh: rows: 16 (over z, y, core), rep: 2 (over x).
Axes of the slice: x: 2, y: 2, z: 4, core: 2. Of those that a mesh axis runs over, the one named last changes fastest.
Arguments:
- embeddings: bfloat16 [11264, 1024], P(('rows', 'rep')), may hold values from -6 to 6
- owner_ids: int32 [11264, 1], P(('rows', 'rep')), may hold values from 0 to 15; in each aligned block of 352 rows (0 to 351, 352 to 703, ...) at most 64 rows name the same one
- live_mask: int32 [11264], P(('rows', 'rep')), may hold values 0 or 1
Outputs:
- neighbour_means: bfloat16 [11264, 1024], P(('rows', 'rep'))
Inputs may be any that keep to these rules, and one draw needn't show every extreme that they name: `owner_ids`: among the rows of one device, at most 64 name the same owner, and in every draw some owner is named by exactly 64 of them.
All inputs are finite; a program needn't handle non-finite values. Where the computation divides by a largest or mean magnitude, that divisor is 1e-20 or more. No bound on the sum of `live_mask` on one device may be relied on, other than what follows from the above.
Results may differ from a plain program's by a relative error of at most 0.0017.
The roundings to bfloat16 on the way count: a program that leaves them out, or rounds other values in their place, can miss the bound.
Values may be sent and summed in bfloat16 or wider, within the bound.
A program may use at most 64 MiB of HBM per device.

v0:
```python
import jax
import jax.numpy as jnp
from jax import lax
from jax.sharding import PartitionSpec as P

BUCKET = 1024
JOIN_ROWS = 8192
KERNEL_SCALE = 4.0
EPSILON = 1e-06
SPLIT = lax.Precision.HIGH
PRECISE = lax.Precision.HIGHEST


def block_positions(owner_block, owners, slot_cap):
    rows = owner_block.shape[0]
    same = owner_block[:, None] == owner_block[None, :]
    index = jnp.arange(rows, dtype=jnp.int32)
    earlier = index[None, :] < index[:, None]
    slot_rank = jnp.sum((same & earlier).astype(jnp.int32), axis=1)
    return owner_block * slot_cap + slot_rank


def whiten(embedded, inverse_root):
    mapped = jnp.dot(embedded, inverse_root, preferred_element_type=jnp.float32)
    return (mapped * lax.rsqrt(jnp.mean(mapped * mapped, axis=1, keepdims=True) + EPSILON)).astype(
        jnp.bfloat16
    )


def root_of(moment):
    y = moment / jnp.max(jnp.sum(jnp.abs(moment), axis=1))
    eye = jnp.eye(y.shape[0], dtype=jnp.float32)
    square = jnp.dot(y, y, precision=SPLIT)
    inner = 1.6875 * eye - 0.5625 * y + 0.0625 * square
    return (2.25 * eye - 2.4375 * y + jnp.dot(square, inner, precision=SPLIT)).astype(jnp.bfloat16)


def masked_means(queries, members, same, alive):
    scores = lax.dot_general(
        queries, members, (((1,), (1,)), ((), ())), preferred_element_type=jnp.float32
    )
    weights = jnp.where(same, jnp.exp(KERNEL_SCALE * (scores / members.shape[1] - 1.0)), 0.0)
    denominator = jnp.sum(weights, axis=1, keepdims=True)
    summed = jnp.dot(weights.astype(jnp.bfloat16), members, preferred_element_type=jnp.float32)
    averaged = summed / jnp.where(alive[:, None] > 0, denominator, 1.0)
    normed = averaged * lax.rsqrt(jnp.mean(averaged * averaged, axis=1, keepdims=True) + EPSILON)
    return (normed * alive[:, None]).astype(jnp.bfloat16)


def spread(values, positions, slots_all):
    return jnp.zeros((slots_all,) + values.shape[1:], values.dtype).at[positions].set(values)


def by_exchange(embeddings, owner_ids, live_mask):
    rows_here, columns = embeddings.shape
    owners = lax.axis_size("rows")
    slot_cap = BUCKET // owners
    positions = block_positions(owner_ids[:, 0], owners, slot_cap)
    live_rows = live_mask.astype(jnp.bfloat16)
    masked = embeddings * live_rows[:, None]
    partial_moment = lax.dot_general(
        masked, masked, (((0,), (0,)), ((), ())), preferred_element_type=jnp.float32
    )
    inverse_root = root_of(lax.psum(partial_moment, ("rows", "rep")))
    whitened = whiten(embeddings, inverse_root)

    def swapped(values):
        return lax.all_to_all(values, "rows", split_axis=0, concat_axis=0, tiled=True)

    members = swapped(
        spread(whitened, positions, BUCKET).reshape(owners, slot_cap, columns)
    ).reshape(BUCKET, columns)
    alive = swapped(spread(live_rows, positions, BUCKET).reshape(owners, slot_cap))
    alive = alive.reshape(BUCKET).astype(jnp.float32)
    means = masked_means(members, members, alive[None, :] > 0, alive)
    returned = swapped(means.reshape(owners, slot_cap, columns))
    return returned.reshape(BUCKET, columns)[positions]


def by_gather(embeddings, owner_ids, live_mask):
    rows_here, columns = embeddings.shape
    owners = lax.axis_size("rows")
    key = jnp.where(live_mask > 0, owner_ids[:, 0], -1)
    keys = lax.all_gather(key, "rows", axis=0, tiled=True)
    everyone = lax.all_gather(embeddings, "rows", axis=0, tiled=True)
    share = columns // owners
    masked = everyone * (keys >= 0).astype(jnp.bfloat16)[:, None]
    own = lax.dynamic_slice_in_dim(masked, lax.axis_index("rows") * share, share, 1)
    part = lax.dot_general(
        own, masked, (((0,), (0,)), ((), ())), preferred_element_type=jnp.float32
    )
    part = lax.psum(part, "rep")
    moment = lax.all_gather(part, "rows", axis=0, tiled=True)
    whitened = whiten(everyone, root_of(moment))
    mine = lax.dynamic_slice_in_dim(whitened, lax.axis_index("rows") * rows_here, rows_here, 0)
    alive = (live_mask > 0).astype(jnp.float32)
    return masked_means(mine, whitened, owner_ids == keys[None, :], alive)


def solution(mesh):
    placed = (P(("rows", "rep"), None), P(("rows", "rep"), None), P(("rows", "rep")))

    def per_device(embeddings, owner_ids, live_mask):
        gathered = embeddings.shape[0] * mesh.shape["rows"]
        join = by_gather if gathered <= JOIN_ROWS else by_exchange
        return join(embeddings, owner_ids, live_mask)

    return jax.shard_map(
        per_device, mesh=mesh, in_specs=placed, out_specs=P(("rows", "rep"), None), check_vma=False
    )
```

profile of v0, /device:TPU:0, one launch (start us, length us, event | category | flops | bytes accessed | tf_op | source)
XLA Modules:
  0.0 265.8 jit_solution(3059865663002023440)
XLA Ops:
  6.5 0.7 all-gather.3.cloned.1.call-update
  7.3 0.0 all-reduce.3.cloned.1.call-start
  7.3 0.7 reduce.1
  8.0 1.2 dynamic-slice.4
  9.9 0.7 fusion.31
  10.6 0.1 select_dynamic-update-slice_fusion
  10.7 65.3 %all-reduce = s32[5632]{0:T(1024)S(1)} all-reduce(s32[5632]{0:T(1024)S(1)} %select_dynamic-update-slice_fusion), channel_id=1, replica_groups=mesh['rows'=16,'rep'=2] {'rows'}, use_global_device_ids=true, to_apply=%add | all-reduce | flops 5632 | bytes 45056
  76.0 31.2 %all-gather.3.cloned.1.call-done = bf16[5632,1024]{1,0:T(8,128)(2,1)} async-done(((bf16[352,1024]{1,0:T(8,128)(2,1)}), bf16[5632,1024]{1,0:T(8,128)(2,1)}) %all-gather.3.cloned.1.call-update) | async-done | bytes 11534352 | tf_op jit(solution)/shard_map/all_gather | solution.py:85
  107.2 7.0 %broadcast_multiply_fusion = bf16[5632,1024]{1,0:T(8,128)(2,1)S(1)} fusion(bf16[5632,1024]{1,0:T(8,128)(2,1)} %all-gather.3.cloned.1.call-done, bf16[5632]{0:T(1024)(128)(2,1)S(1)} %compare_convert_fusion), kind=kLoop, calls=%fused_computation.7 | loop fusion | flops 5767168 | bytes 23079936 | tf_op jit(solution)/shard_map/mul | solution.py:87
  114.2 3.3 %fusion.19 = f32[64,1024]{1,0:T(8,128)} fusion(bf16[5632,1024]{1,0:T(8,128)(2,1)S(1)} %broadcast_multiply_fusion, s32[]{:T(128)S(6)} %select_n.20), kind=kOutput, calls=%fused_computation.27 | convolution fusion | flops 738197504 | bytes 13238276 | tf_op jit(solution)/shard_map/dot_general | solution.py:89
  117.5 0.0 all-reduce.3.cloned.1.call-update
  117.5 0.0 all-gather.5.cloned.1.call-start
  117.6 21.7 %all-reduce.3.cloned.1.call-done = f32[64,1024]{1,0:T(8,128)} async-done(((f32[64,1024]{1,0:T(8,128)}), f32[64,1024]{1,0:T(8,128)}) %all-reduce.3.cloned.1.call-update) | async-done | bytes 262160 | tf_op jit(solution)/shard_map/psum | solution.py:92
  139.3 0.0 all-gather.5.cloned.1.call-update
  139.3 53.0 %all-gather.5.cloned.1.call-done = f32[1024,1024]{1,0:T(8,128)} async-done(((f32[64,1024]{1,0:T(8,128)}), f32[1024,1024]{1,0:T(8,128)}) %all-gather.5.cloned.1.call-update) | async-done | bytes 4194320 | tf_op jit(solution)/shard_map/all_gather | solution.py:93
  192.3 2.6 abs_reduce_fusion
  194.8 0.6 reduce_max.9
  195.4 11.7 %fusion.18 = f32[1024,1024]{1,0:T(8,128)S(1)} fusion(f32[1024,1024]{1,0:T(8,128)} %all-gather.5.cloned.1.call-done, f32[]{:T(128)} %reduce_max.9), kind=kOutput, calls=%fused_computation.24 | convolution fusion | flops 6443499520 | bytes 8388612 | tf_op jit(solution)/shard_map/dot_general | solution.py:33
  207.2 8.6 %add_convert_fusion = bf16[1024,1024]{1,0:T(8,128)(2,1)S(1)} fusion(f32[1024,1024]{1,0:T(8,128)S(1)} %fusion.18, f32[1024,1024]{1,0:T(8,128)S(1)} %copy-done, f32[]{:T(128)} %reduce_max.9), kind=kOutput, calls=%fused_computation.8 | convolution fusion | flops 6457131008 | bytes 10485764 | tf_op jit(solution)/shard_map/dot_general | solution.py:35
  215.8 19.5 %multiply_reduce_fusion = (f32[5632]{0:T(1024)S(1)}, f32[1024,5632]{1,0:T(8,128)}) fusion(bf16[1024,1024]{1,0:T(8,128)(2,1)S(1)} %add_convert_fusion, bf16[5632,1024]{1,0:T(8,128)(2,1)} %all-gather.3.cloned.1.call-done), kind=kOutput, calls=%fused_computation.1 | convolution fusion | flops 11822688256 | bytes 36722688 | tf_op jit(solution)/shard_map/dot_general | solution.py:24
  235.3 8.7 %multiply_convert_fusion = bf16[1024,5632]{1,0:T(8,128)(2,1)S(1)} fusion(f32[1024,5632]{1,0:T(8,128)} %get-tuple-element.8, f32[5632]{0:T(1024)S(1)} %add_rsqrt_fusion), kind=kLoop, calls=%fused_computation | loop fusion | flops 11534336 | bytes 34625536 | tf_op jit(solution)/shard_map/convert_element_type | solution.py:25
  244.0 7.7 %fusion.32 = (f32[352]{0:T(512)S(1)}, bf16[352,5632]{1,0:T(8,128)(2,1)}) fusion(bf16[1024,5632]{1,0:T(8,128)(2,1)S(1)} %multiply_convert_fusion, s32[]{:T(128)S(6)} %select_n.21, s32[5632]{0:T(1024)S(1)} %all-reduce, s32[352]{0:T(512)S(1)} %reduce.1), kind=kOutput, calls=%fused_computation.44 | convolution fusion | flops 4073963264 | bytes 16313732 | tf_op jit(solution)/shard_map/dot_general | solution.py:39
  251.7 6.5 %multiply_reduce_fusion.1 = (f32[352]{0:T(512)S(1)}, f32[352,1024]{1,0:T(8,128)S(1)}) fusion(f32[352]{0:T(512)S(1)} %compare_select_fusion, bf16[1024,5632]{1,0:T(8,128)(2,1)S(1)} %multiply_convert_fusion, bf16[352,5632]{1,0:T(8,128)(2,1)} %get-tuple-element.10), kind=kOutput, calls=%fused_computation.26 | convolution fusion | flops 4061167360 | bytes 16943872 | tf_op jit(solution)/shard_map/dot_general | solution.py:44
  258.2 1.1 multiply_convert_fusion.1
  (8 shorter events, 0.0 us)
Async XLA Ops:
  6.5 100.7 %all-gather.3.cloned.1.call-start = ((), (), s32[]{:S(2)}) async-start(), calls=%async_computation | async-start | bytes 12255232 | tf_op jit(solution)/shard_map/all_gather | solution.py:85
  7.3 132.0 %all-reduce.3.cloned.1.call-start = ((), (), s32[]{:S(2)}) async-start(), calls=%async_computation.1 | async-start | bytes 524288 | tf_op jit(solution)/shard_map/psum | solution.py:92
  117.5 74.8 %all-gather.5.cloned.1.call-start = ((), (), s32[]{:S(2)}) async-start(), calls=%async_computation.2 | async-start | bytes 4456448 | tf_op jit(solution)/shard_map/all_gather | solution.py:93
  195.4 11.7 %copy-start = (f32[1024,1024]{1,0:T(8,128)S(1)}, f32[1024,1024]{1,0:T(8,128)}, u32[]{:S(2)}) copy-start(f32[1024,1024]{1,0:T(8,128)} %all-gather.5.cloned.1.call-done) | copy-start | bytes 12582916
Sparse Core Ops, SparseCore 0:
  9.6 97.5 all-gather.2
  117.6 21.6 all-reduce.2
  141.7 50.5 all-gather.4
where the time goes:
time: 266 us
  waiting for transfers between devices  107 us (40%)
  blocking collectives  65.3 us (25%)
  matrix products  57.3 us (22%)
  other arithmetic  21.4 us (8%)
  between operations  13.8 us (5%)
    unnamed x1, blocking collectives  65.3 us
    all_gather x1, waiting for transfers between devices, by_gather(): moment = lax.all_gather(part, 'rows', axis=0, tiled=True)  53 us
    all_gather x1, waiting for transfers between devices, by_gather(): everyone = lax.all_gather(embeddings, 'rows', axis=0, tiled=True)  31.2 us
    psum x1, waiting for transfers between devices, by_gather(): part = lax.psum(part, 'rep')  21.7 us
    dot_general x1, matrix products, whiten(): mapped = jnp.dot(embedded, inverse_root, preferred_element_type=jnp.float32)  19.5 us
    dot_general x1, matrix products, root_of(): square = jnp.dot(y, y, precision=SPLIT)  11.7 us
    convert_element_type x1, other arithmetic, whiten(): (mapped * lax.rsqrt(jnp.mean(mapped * mapped, axis=1, keepdims=True) + EP...  8.69 us
    dot_general x1, matrix products, root_of(): jnp.dot(square, inner, precision=SPLIT)  8.6 us
  transfers between devices with their start and end apart: 3, of which 3 were waited for; matrix products, arithmetic and copies ran while one was open for 1% of the time, Pallas kernels for 0%

commit v1 on v0

--- a/solution.py
+++ b/solution.py
@@ -90,7 +90,21 @@
         own, masked, (((0,), (0,)), ((), ())), preferred_element_type=jnp.float32
     )
     part = lax.psum(part, "rep")
-    moment = lax.all_gather(part, "rows", axis=0, tiled=True)
+    ways, here, turn = (lax.axis_size("rows"), lax.axis_index("rows"), part.shape[0])
+    shape = [n * ways if d == 0 else n for d, n in enumerate(part.shape)]
+    full = lax.dynamic_update_slice_in_dim(jnp.zeros(shape, part.dtype), part, here * turn, axis=0)
+    going_up = going_down = part
+    for far in range(1, ways // 2 + 1):
+        going_up = lax.ppermute(going_up, "rows", [(d, (d + 1) % ways) for d in range(ways)])
+        full = lax.dynamic_update_slice_in_dim(full, going_up, (here - far) % ways * turn, axis=0)
+        if 2 * far < ways:
+            going_down = lax.ppermute(
+                going_down, "rows", [(d, (d - 1) % ways) for d in range(ways)]
+            )
+            full = lax.dynamic_update_slice_in_dim(
+                full, going_down, (here + far) % ways * turn, axis=0
+            )
+    moment = full
     whitened = whiten(everyone, root_of(moment))
     mine = lax.dynamic_slice_in_dim(whitened, lax.axis_index("rows") * rows_here, rows_here, 0)
     alive = (live_mask > 0).astype(jnp.float32)

time: 266 us -> 282 us (1.060)
  starting transfers between devices: 0.08 us -> 32 us
  waiting for transfers between devices: 107 us -> 89.8 us
    all_gather x1 -> x0, waiting for transfers between devices: 53 us -> none  [by_gather(): moment = lax.all_gather(part, 'rows', axis=0, tiled=True)]
    ppermute x0 -> x15, waiting for transfers between devices: none -> 36 us  [the longest x8 34.6 us: by_gather(): lax.ppermute(going_up, 'rows', [(d, (d + 1) % ways) for d in range(ways)])]
    ppermute x0 -> x15, starting transfers between devices: none -> 32 us  [the longest x7 31.9 us: by_gather(): lax.ppermute(going_down, 'rows', [(d, (d - 1) % ways) for d in range(ways)])]
  transfers between devices with their start and end apart: 3 -> 17, of which waited for: 3 -> 14; matrix products, arithmetic and copies ran while one was open for 1% -> 1% of each run, Pallas kernels for 0% -> 0%
where the time goes in v1:
time: 282 us
  waiting for transfers between devices  89.8 us (32%)
  blocking collectives  65.2 us (23%)
  matrix products  57.5 us (20%)
  starting transfers between devices  32 us (11%)
  other arithmetic  19.2 us (7%)
  between operations  14.2 us (5%)
  local copies, waits for them, and re-layouts  4.05 us (1%)
    unnamed x1, blocking collectives  65.2 us
    ppermute x8, waiting for transfers between devices, by_gather(): lax.ppermute(going_up, 'rows', [(d, (d + 1) % ways) for d in range(ways)])  34.6 us
    ppermute x7, starting transfers between devices, by_gather(): lax.ppermute(going_down, 'rows', [(d, (d - 1) % ways) for d in range(ways)])  31.9 us
    all_gather x1, waiting for transfers between devices, by_gather(): everyone = lax.all_gather(embeddings, 'rows', axis=0, tiled=True)  31.4 us
    psum x1, waiting for transfers between devices, by_gather(): part = lax.psum(part, 'rep')  21.8 us
    dot_general x1, matrix products, whiten(): mapped = jnp.dot(embedded, inverse_root, preferred_element_type=jnp.float32)  19.6 us
    dot_general x1, matrix products, root_of(): square = jnp.dot(y, y, precision=SPLIT)  11.7 us
    convert_element_type x1, other arithmetic, whiten(): (mapped * lax.rsqrt(jnp.mean(mapped * mapped, axis=1, keepdims=True) + EP...  8.69 us
  transfers between devices with their start and end apart: 17, of which 14 were waited for; matrix products, arithmetic and copies ran while one was open for 1% of the time, Pallas kernels for 0%

profile of v1, /device:TPU:0, one launch (start us, length us, event | category | flops | bytes accessed | tf_op | source)
XLA Modules:
  0.0 282.0 jit_solution(8569070241585897082)
XLA Ops:
  10.7 65.2 %all-reduce = s32[5632]{0:T(1024)S(1)} all-reduce(s32[5632]{0:T(1024)S(1)} %select_dynamic-update-slice_fusion), channel_id=1, replica_groups=mesh['rows'=16,'rep'=2] {'rows'}, use_global_device_ids=true, to_apply=%add | all-reduce | flops 5632 | bytes 45056
  75.9 31.4 %all-gather.2.cloned.1.call-done = bf16[5632,1024]{1,0:T(8,128)(2,1)} async-done(((bf16[352,1024]{1,0:T(8,128)(2,1)}), bf16[5632,1024]{1,0:T(8,128)(2,1)}) %all-gather.2.cloned.1.call-update) | async-done | bytes 11534352 | tf_op jit(solution)/shard_map/all_gather | solution.py:85
  107.2 7.0 %broadcast_multiply_fusion = bf16[5632,1024]{1,0:T(8,128)(2,1)S(1)} fusion(bf16[5632,1024]{1,0:T(8,128)(2,1)} %all-gather.2.cloned.1.call-done, bf16[5632]{0:T(1024)(128)(2,1)S(1)} %compare_convert_fusion), kind=kLoop, calls=%fused_computation.7 | loop fusion | flops 5767168 | bytes 23079936 | tf_op jit(solution)/shard_map/mul | solution.py:87
  117.5 21.8 %all-reduce.3.cloned.1.call-done = f32[64,1024]{1,0:T(8,128)} async-done(((f32[64,1024]{1,0:T(8,128)}), f32[64,1024]{1,0:T(8,128)}) %all-reduce.3.cloned.1.call-update) | async-done | bytes 262160 | tf_op jit(solution)/shard_map/psum | solution.py:92
  139.3 4.4 %collective-permute-start.1 = (f32[64,1024]{1,0:T(8,128)}, f32[64,1024]{1,0:T(8,128)S(1)}, u32[]{:S(2)}, u32[]{:S(2)}) collective-permute-start(f32[64,1024]{1,0:T(8,128)} %all-reduce.3.cloned.1.call-done), channel_id=1, source_target_pairs={{0,30},{2,0},{4,2},{6,4},{8,6},{10,8},{12,10},{14,12},{16,14},{18,... | collective-permute-start | bytes 786440 | tf_op jit(solution)/shard_map/ppermute | solution.py:101
  143.7 4.4 %collective-permute-done = f32[64,1024]{1,0:T(8,128)S(1)} collective-permute-done((f32[64,1024]{1,0:T(8,128)}, f32[64,1024]{1,0:T(8,128)S(1)}, u32[]{:S(2)}, u32[]{:S(2)}) %collective-permute-start) | collective-permute-done | bytes 262176 | tf_op jit(solution)/shard_map/ppermute | solution.py:98
  148.1 4.4 %collective-permute-start.3 = (f32[64,1024]{1,0:T(8,128)S(1)}, f32[64,1024]{1,0:T(8,128)S(1)}, u32[]{:S(2)}, u32[]{:S(2)}) collective-permute-start(f32[64,1024]{1,0:T(8,128)S(1)} %collective-permute-done.1), channel_id=1, source_target_pairs={{0,30},{2,0},{4,2},{6,4},{8,6},{10,8},{12,10},{14,12},{16,14},{18,... | collective-permute-start | bytes 786440 | tf_op jit(solution)/shard_map/ppermute | solution.py:101
  152.5 4.2 %collective-permute-done.2 = f32[64,1024]{1,0:T(8,128)S(1)} collective-permute-done((f32[64,1024]{1,0:T(8,128)S(1)}, f32[64,1024]{1,0:T(8,128)S(1)}, u32[]{:S(2)}, u32[]{:S(2)}) %collective-permute-start.2) | collective-permute-done | bytes 262176 | tf_op jit(solution)/shard_map/ppermute | solution.py:98
  156.7 4.4 %collective-permute-start.5 = (f32[64,1024]{1,0:T(8,128)S(1)}, f32[64,1024]{1,0:T(8,128)S(1)}, u32[]{:S(2)}, u32[]{:S(2)}) collective-permute-start(f32[64,1024]{1,0:T(8,128)S(1)} %collective-permute-done.3), channel_id=1, source_target_pairs={{0,30},{2,0},{4,2},{6,4},{8,6},{10,8},{12,10},{14,12},{16,14},{18,... | collective-permute-start | bytes 786440 | tf_op jit(solution)/shard_map/ppermute | solution.py:101
  161.1 4.2 %collective-permute-done.4 = f32[64,1024]{1,0:T(8,128)S(1)} collective-permute-done((f32[64,1024]{1,0:T(8,128)S(1)}, f32[64,1024]{1,0:T(8,128)S(1)}, u32[]{:S(2)}, u32[]{:S(2)}) %collective-permute-start.4) | collective-permute-done | bytes 262176 | tf_op jit(solution)/shard_map/ppermute | solution.py:98
  165.9 4.5 %collective-permute-start.7 = (f32[64,1024]{1,0:T(8,128)S(1)}, f32[64,1024]{1,0:T(8,128)S(1)}, u32[]{:S(2)}, u32[]{:S(2)}) collective-permute-start(f32[64,1024]{1,0:T(8,128)S(1)} %collective-permute-done.5), channel_id=1, source_target_pairs={{0,30},{2,0},{4,2},{6,4},{8,6},{10,8},{12,10},{14,12},{16,14},{18,... | collective-permute-start | bytes 786440 | tf_op jit(solution)/shard_map/ppermute | solution.py:101
  170.4 3.5 %collective-permute-done.6 = f32[64,1024]{1,0:T(8,128)S(1)} collective-permute-done((f32[64,1024]{1,0:T(8,128)S(1)}, f32[64,1024]{1,0:T(8,128)S(1)}, u32[]{:S(2)}, u32[]{:S(2)}) %collective-permute-start.6) | collective-permute-done | bytes 262176 | tf_op jit(solution)/shard_map/ppermute | solution.py:98
  174.3 4.7 %collective-permute-start.9 = (f32[64,1024]{1,0:T(8,128)S(1)}, f32[64,1024]{1,0:T(8,128)S(1)}, u32[]{:S(2)}, u32[]{:S(2)}) collective-permute-start(f32[64,1024]{1,0:T(8,128)S(1)} %collective-permute-done.7), channel_id=1, source_target_pairs={{0,30},{2,0},{4,2},{6,4},{8,6},{10,8},{12,10},{14,12},{16,14},{18,... | collective-permute-start | bytes 786440 | tf_op jit(solution)/shard_map/ppermute | solution.py:101
  179.0 3.5 %collective-permute-done.8 = f32[64,1024]{1,0:T(8,128)S(1)} collective-permute-done((f32[64,1024]{1,0:T(8,128)S(1)}, f32[64,1024]{1,0:T(8,128)S(1)}, u32[]{:S(2)}, u32[]{:S(2)}) %collective-permute-start.8) | collective-permute-done | bytes 262176 | tf_op jit(solution)/shard_map/ppermute | solution.py:98
  182.9 4.7 %collective-permute-start.11 = (f32[64,1024]{1,0:T(8,128)S(1)}, f32[64,1024]{1,0:T(8,128)S(1)}, u32[]{:S(2)}, u32[]{:S(2)}) collective-permute-start(f32[64,1024]{1,0:T(8,128)S(1)} %collective-permute-done.9), channel_id=1, source_target_pairs={{0,30},{2,0},{4,2},{6,4},{8,6},{10,8},{12,10},{14,12},{16,14},{18,... | collective-permute-start | bytes 786440 | tf_op jit(solution)/shard_map/ppermute | solution.py:101
  187.6 3.5 %collective-permute-done.10 = f32[64,1024]{1,0:T(8,128)S(1)} collective-permute-done((f32[64,1024]{1,0:T(8,128)S(1)}, f32[64,1024]{1,0:T(8,128)S(1)}, u32[]{:S(2)}, u32[]{:S(2)}) %collective-permute-start.10) | collective-permute-done | bytes 262176 | tf_op jit(solution)/shard_map/ppermute | solution.py:98
  191.5 4.7 %collective-permute-start.13 = (f32[64,1024]{1,0:T(8,128)S(1)}, f32[64,1024]{1,0:T(8,128)S(1)}, u32[]{:S(2)}, u32[]{:S(2)}) collective-permute-start(f32[64,1024]{1,0:T(8,128)S(1)} %collective-permute-done.11), channel_id=1, source_target_pairs={{0,30},{2,0},{4,2},{6,4},{8,6},{10,8},{12,10},{14,12},{16,14},{18,... | collective-permute-start | bytes 786440 | tf_op jit(solution)/shard_map/ppermute | solution.py:101
  200.1 8.1 %collective-permute-done.14 = f32[64,1024]{1,0:T(8,128)S(1)} collective-permute-done((f32[64,1024]{1,0:T(8,128)S(1)}, f32[64,1024]{1,0:T(8,128)S(1)}, u32[]{:S(2)}, u32[]{:S(2)}) %collective-permute-start.14) | collective-permute-done | bytes 262176 | tf_op jit(solution)/shard_map/ppermute | solution.py:98
  211.1 11.7 %fusion.18 = f32[1024,1024]{1,0:T(8,128)S(1)} fusion(f32[1024,1024]{1,0:T(8,128)} %copy-done, f32[]{:T(128)} %reduce_max.9), kind=kOutput, calls=%fused_computation.24 | convolution fusion | flops 6443499520 | bytes 8388612 | tf_op jit(solution)/shard_map/dot_general | solution.py:33
  222.9 8.6 %add_convert_fusion = bf16[1024,1024]{1,0:T(8,128)(2,1)S(1)} fusion(f32[1024,1024]{1,0:T(8,128)S(1)} %fusion.18, f32[1024,1024]{1,0:T(8,128)S(1)} %copy-done.1, f32[]{:T(128)} %reduce_max.9), kind=kOutput, calls=%fused_computation.8 | convolution fusion | flops 6457131008 | bytes 10485764 | tf_op jit(solution)/shard_map/dot_general | solution.py:35
  231.5 19.6 %multiply_reduce_fusion = (f32[5632]{0:T(1024)S(1)}, f32[1024,5632]{1,0:T(8,128)}) fusion(bf16[1024,1024]{1,0:T(8,128)(2,1)S(1)} %add_convert_fusion, bf16[5632,1024]{1,0:T(8,128)(2,1)} %all-gather.2.cloned.1.call-done), kind=kOutput, calls=%fused_computation.1 | convolution fusion | flops 11822688256 | bytes 36722688 | tf_op jit(solution)/shard_map/dot_general | solution.py:24
  251.1 8.7 %multiply_convert_fusion = bf16[1024,5632]{1,0:T(8,128)(2,1)S(1)} fusion(f32[1024,5632]{1,0:T(8,128)} %get-tuple-element.8, f32[5632]{0:T(1024)S(1)} %add_rsqrt_fusion), kind=kLoop, calls=%fused_computation | loop fusion | flops 11534336 | bytes 34625536 | tf_op jit(solution)/shard_map/convert_element_type | solution.py:25
  259.8 7.7 %fusion.32 = (f32[352]{0:T(512)S(1)}, bf16[352,5632]{1,0:T(8,128)(2,1)}) fusion(bf16[1024,5632]{1,0:T(8,128)(2,1)S(1)} %multiply_convert_fusion, s32[]{:T(128)S(6)} %select_n.160, s32[5632]{0:T(1024)S(1)} %all-reduce, s32[352]{0:T(512)S(1)} %reduce.1), kind=kOutput, calls=%fused_computation.60 | convolution fusion | flops 4073963264 | bytes 16313732 | tf_op jit(solution)/shard_map/dot_general | solution.py:39
  267.6 6.5 %multiply_reduce_fusion.1 = (f32[352]{0:T(512)S(1)}, f32[352,1024]{1,0:T(8,128)S(1)}) fusion(f32[352]{0:T(512)S(1)} %compare_select_fusion, bf16[1024,5632]{1,0:T(8,128)(2,1)S(1)} %multiply_convert_fusion, bf16[352,5632]{1,0:T(8,128)(2,1)} %get-tuple-element.10), kind=kOutput, calls=%fused_computation.26 | convolution fusion | flops 4061167360 | bytes 16943872 | tf_op jit(solution)/shard_map/dot_general | solution.py:44
  (56 shorter events, 16.5 us)
Async XLA Ops:
  6.5 100.7 %all-gather.2.cloned.1.call-start = ((), (), s32[]{:S(2)}) async-start(), calls=%async_computation | async-start | bytes 12255232 | tf_op jit(solution)/shard_map/all_gather | solution.py:85
  7.3 132.0 %all-reduce.3.cloned.1.call-start = ((), (), s32[]{:S(2)}) async-start(), calls=%async_computation.1 | async-start | bytes 524288 | tf_op jit(solution)/shard_map/psum | solution.py:92
  139.3 26.5 %copy-start.2 = (f32[64,1024]{1,0:T(8,128)S(1)}, f32[64,1024]{1,0:T(8,128)}, u32[]{:S(2)}) copy-start(f32[64,1024]{1,0:T(8,128)} %all-reduce.3.cloned.1.call-done) | copy-start | bytes 786436
  139.3 8.8 %collective-permute-start = (f32[64,1024]{1,0:T(8,128)}, f32[64,1024]{1,0:T(8,128)S(1)}, u32[]{:S(2)}, u32[]{:S(2)}) collective-permute-start(f32[64,1024]{1,0:T(8,128)} %all-reduce.3.cloned.1.call-done), channel_id=1, source_target_pairs={{0,2},{2,4},{4,6},{6,8},{8,10},{10,12},{12,14},{14,16},{16,18},{18... | collective-permute-start | bytes 786440 | tf_op jit(solution)/shard_map/ppermute | solution.py:98
  139.3 8.8 %collective-permute-start.1 = (f32[64,1024]{1,0:T(8,128)}, f32[64,1024]{1,0:T(8,128)S(1)}, u32[]{:S(2)}, u32[]{:S(2)}) collective-permute-start(f32[64,1024]{1,0:T(8,128)} %all-reduce.3.cloned.1.call-done), channel_id=1, source_target_pairs={{0,30},{2,0},{4,2},{6,4},{8,6},{10,8},{12,10},{14,12},{16,14},{18,... | collective-permute-start | bytes 786440 | tf_op jit(solution)/shard_map/ppermute | solution.py:101
  148.1 8.6 %collective-permute-start.2 = (f32[64,1024]{1,0:T(8,128)S(1)}, f32[64,1024]{1,0:T(8,128)S(1)}, u32[]{:S(2)}, u32[]{:S(2)}) collective-permute-start(f32[64,1024]{1,0:T(8,128)S(1)} %collective-permute-done), channel_id=1, source_target_pairs={{0,2},{2,4},{4,6},{6,8},{8,10},{10,12},{12,14},{14,16},{16,18},{18... | collective-permute-start | bytes 786440 | tf_op jit(solution)/shard_map/ppermute | solution.py:98
  148.1 8.6 %collective-permute-start.3 = (f32[64,1024]{1,0:T(8,128)S(1)}, f32[64,1024]{1,0:T(8,128)S(1)}, u32[]{:S(2)}, u32[]{:S(2)}) collective-permute-start(f32[64,1024]{1,0:T(8,128)S(1)} %collective-permute-done.1), channel_id=1, source_target_pairs={{0,30},{2,0},{4,2},{6,4},{8,6},{10,8},{12,10},{14,12},{16,14},{18,... | collective-permute-start | bytes 786440 | tf_op jit(solution)/shard_map/ppermute | solution.py:101
  156.7 8.6 %collective-permute-start.4 = (f32[64,1024]{1,0:T(8,128)S(1)}, f32[64,1024]{1,0:T(8,128)S(1)}, u32[]{:S(2)}, u32[]{:S(2)}) collective-permute-start(f32[64,1024]{1,0:T(8,128)S(1)} %collective-permute-done.2), channel_id=1, source_target_pairs={{0,2},{2,4},{4,6},{6,8},{8,10},{10,12},{12,14},{14,16},{16,18},{18... | collective-permute-start | bytes 786440 | tf_op jit(solution)/shard_map/ppermute | solution.py:98
  156.7 9.2 %collective-permute-start.5 = (f32[64,1024]{1,0:T(8,128)S(1)}, f32[64,1024]{1,0:T(8,128)S(1)}, u32[]{:S(2)}, u32[]{:S(2)}) collective-permute-start(f32[64,1024]{1,0:T(8,128)S(1)} %collective-permute-done.3), channel_id=1, source_target_pairs={{0,30},{2,0},{4,2},{6,4},{8,6},{10,8},{12,10},{14,12},{16,14},{18,... | collective-permute-start | bytes 786440 | tf_op jit(solution)/shard_map/ppermute | solution.py:101
  165.3 8.6 %collective-permute-start.6 = (f32[64,1024]{1,0:T(8,128)S(1)}, f32[64,1024]{1,0:T(8,128)S(1)}, u32[]{:S(2)}, u32[]{:S(2)}) collective-permute-start(f32[64,1024]{1,0:T(8,128)S(1)} %collective-permute-done.4), channel_id=1, source_target_pairs={{0,2},{2,4},{4,6},{6,8},{8,10},{10,12},{12,14},{14,16},{16,18},{18... | collective-permute-start | bytes 786440 | tf_op jit(solution)/shard_map/ppermute | solution.py:98
  165.9 8.4 %collective-permute-start.7 = (f32[64,1024]{1,0:T(8,128)S(1)}, f32[64,1024]{1,0:T(8,128)S(1)}, u32[]{:S(2)}, u32[]{:S(2)}) collective-permute-start(f32[64,1024]{1,0:T(8,128)S(1)} %collective-permute-done.5), channel_id=1, source_target_pairs={{0,30},{2,0},{4,2},{6,4},{8,6},{10,8},{12,10},{14,12},{16,14},{18,... | collective-permute-start | bytes 786440 | tf_op jit(solution)/shard_map/ppermute | solution.py:101
  173.9 8.6 %collective-permute-start.8 = (f32[64,1024]{1,0:T(8,128)S(1)}, f32[64,1024]{1,0:T(8,128)S(1)}, u32[]{:S(2)}, u32[]{:S(2)}) collective-permute-start(f32[64,1024]{1,0:T(8,128)S(1)} %collective-permute-done.6), channel_id=1, source_target_pairs={{0,2},{2,4},{4,6},{6,8},{8,10},{10,12},{12,14},{14,16},{16,18},{18... | collective-permute-start | bytes 786440 | tf_op jit(solution)/shard_map/ppermute | solution.py:98
  174.3 8.6 %collective-permute-start.9 = (f32[64,1024]{1,0:T(8,128)S(1)}, f32[64,1024]{1,0:T(8,128)S(1)}, u32[]{:S(2)}, u32[]{:S(2)}) collective-permute-start(f32[64,1024]{1,0:T(8,128)S(1)} %collective-permute-done.7), channel_id=1, source_target_pairs={{0,30},{2,0},{4,2},{6,4},{8,6},{10,8},{12,10},{14,12},{16,14},{18,... | collective-permute-start | bytes 786440 | tf_op jit(solution)/shard_map/ppermute | solution.py:101
  182.5 8.6 %collective-permute-start.10 = (f32[64,1024]{1,0:T(8,128)S(1)}, f32[64,1024]{1,0:T(8,128)S(1)}, u32[]{:S(2)}, u32[]{:S(2)}) collective-permute-start(f32[64,1024]{1,0:T(8,128)S(1)} %collective-permute-done.8), channel_id=1, source_target_pairs={{0,2},{2,4},{4,6},{6,8},{8,10},{10,12},{12,14},{14,16},{16,18},{18... | collective-permute-start | bytes 786440 | tf_op jit(solution)/shard_map/ppermute | solution.py:98
  182.9 8.6 %collective-permute-start.11 = (f32[64,1024]{1,0:T(8,128)S(1)}, f32[64,1024]{1,0:T(8,128)S(1)}, u32[]{:S(2)}, u32[]{:S(2)}) collective-permute-start(f32[64,1024]{1,0:T(8,128)S(1)} %collective-permute-done.9), channel_id=1, source_target_pairs={{0,30},{2,0},{4,2},{6,4},{8,6},{10,8},{12,10},{14,12},{16,14},{18,... | collective-permute-start | bytes 786440 | tf_op jit(solution)/shard_map/ppermute | solution.py:101
  191.1 8.6 %collective-permute-start.12 = (f32[64,1024]{1,0:T(8,128)S(1)}, f32[64,1024]{1,0:T(8,128)S(1)}, u32[]{:S(2)}, u32[]{:S(2)}) collective-permute-start(f32[64,1024]{1,0:T(8,128)S(1)} %collective-permute-done.10), channel_id=1, source_target_pairs={{0,2},{2,4},{4,6},{6,8},{8,10},{10,12},{12,14},{14,16},{16,18},{18... | collective-permute-start | bytes 786440 | tf_op jit(solution)/shard_map/ppermute | solution.py:98
  191.5 8.6 %collective-permute-start.13 = (f32[64,1024]{1,0:T(8,128)S(1)}, f32[64,1024]{1,0:T(8,128)S(1)}, u32[]{:S(2)}, u32[]{:S(2)}) collective-permute-start(f32[64,1024]{1,0:T(8,128)S(1)} %collective-permute-done.11), channel_id=1, source_target_pairs={{0,30},{2,0},{4,2},{6,4},{8,6},{10,8},{12,10},{14,12},{16,14},{18,... | collective-permute-start | bytes 786440 | tf_op jit(solution)/shard_map/ppermute | solution.py:101
  199.7 8.5 %collective-permute-start.14 = (f32[64,1024]{1,0:T(8,128)S(1)}, f32[64,1024]{1,0:T(8,128)S(1)}, u32[]{:S(2)}, u32[]{:S(2)}) collective-permute-start(f32[64,1024]{1,0:T(8,128)S(1)} %collective-permute-done.12), channel_id=1, source_target_pairs={{0,2},{2,4},{4,6},{6,8},{8,10},{10,12},{12,14},{14,16},{16,18},{18... | collective-permute-start | bytes 786440 | tf_op jit(solution)/shard_map/ppermute | solution.py:98
  208.2 1.9 copy-start
  211.1 11.7 %copy-start.1 = (f32[1024,1024]{1,0:T(8,128)S(1)}, f32[1024,1024]{1,0:T(8,128)}, u32[]{:S(2)}) copy-start(f32[1024,1024]{1,0:T(8,128)} %copy-done) | copy-start | bytes 12582916
Sparse Core Ops, SparseCore 0:
  9.6 97.5 all-gather.1
  117.6 21.6 all-reduce.2
